TPU v7x, 512 devices: a whole 4x8x8 slice. The times are simulated.
512 devices in a mesh: sub: 128 (over y, z, core), grp: 4 (over x).
Axes of the slice: x: 4, y: 8, z: 8, core: 2. Of those that a mesh axis runs over, the one named last changes fastest.
Arguments:
- gradients: bfloat16 [9, 12, 4, 65536], P(None, None, 'grp', 'sub'), may hold values from -1.75 to 1.75
- moduli: bfloat16 [9, 4, 65536], P(None, 'grp', 'sub'), may hold values from 0.5 to 4
- diag_terms: bfloat16 [12, 4, 65536], P(None, 'grp', 'sub'), may hold values from 0.29882812 to 3
- counts: int32 [4, 128, 128], P('grp', 'sub'), may hold values from 1 to 12, as said below
- targets: int32 [4, 65536], P('grp', 'sub'), may hold values from 0 to 127
- compliance: float32 [144, 4, 16384], P(None, 'grp', 'sub'), as said below
- neighbours: int32 [4, 128, 128], P('grp', 'sub'), may hold values from 0 to 127, each once within a row
- rhs: float32 [12, 4, 16384], P(None, 'grp', 'sub'), may hold values from -6 to 6
Outputs:
- multipliers: float32 [12, 4, 16384], P(None, 'grp', 'sub')
- stiffness: float32 [144, 4, 16384], P(None, 'grp', 'sub')
Inputs may be any that keep to these rules, and one draw needn't show every extreme that they name: Each row counts[g, i, :] sums to 512, every entry is at least 1 and no entry exceeds 12; in every group one owner receives exactly 12 elements from every device of the group. `compliance`: every 12 x 12 block is symmetric positive definite.
All inputs are finite; a program needn't handle non-finite values.
Results may differ from a plain program's by a relative error of at most 0.0003.
Values may be sent and summed in bfloat16 or wider, within the bound.
A program may use at most 64 MiB of HBM per device.

v0:
```python
import jax
import jax.numpy as jnp
from jax import lax
from jax.sharding import PartitionSpec as P

ITERS = 2


def from_behind(block, axis, distance):
    devices = range(lax.axis_size(axis))
    route = [((i - distance) % len(devices), i) for i in devices]
    return lax.ppermute(block, axis, route)


def tangent(grads, moduli_part, extra):
    grads_f = grads.astype(jnp.float32)
    mods_f = moduli_part.astype(jnp.float32)
    blocks = jnp.zeros((12, 12, grads.shape[2]), jnp.float32)
    for entry in range(9):
        weighted = grads_f[entry] * mods_f[entry][None, :]
        blocks = blocks + grads_f[entry][:, None, :] * weighted[None, :, :]
    identity = jnp.eye(12, dtype=jnp.float32)
    blocks = blocks + identity[:, :, None] * extra.astype(jnp.float32)[:, None, :]
    return blocks.reshape(144, -1)


def column_apply(mats, vectors):
    return jnp.sum(mats.reshape(12, 12, -1) * vectors[None], axis=1)


def coupled(mats, vectors, facing, inverse):
    here = column_apply(mats, vectors)
    arrived = from_behind(vectors[:, inverse], "grp", 1)
    there = from_behind(column_apply(mats, arrived), "grp", -1)
    return here + there[:, facing]


def resid_sum(resid, precond):
    return lax.psum(jnp.sum(resid * precond), ("sub", "grp"))


def per_device(gradients, moduli, diag_terms, counts, targets, compliance, neighbours, rhs):
    peers = lax.axis_size("sub")
    elements = targets.shape[1]
    width = compliance.shape[2]
    capacity = 3 * elements // peers
    grads = gradients[:, :, 0, :]
    mods = moduli[:, 0, :]
    extra = diag_terms[:, 0, :]
    peer_counts = counts[0, 0]
    patch_list = targets[0]
    comp = compliance[:, 0, :]
    facing = neighbours[0, 0]
    ends = jnp.cumsum(peer_counts)
    starts = ends - peer_counts
    within = jnp.arange(capacity, dtype=jnp.int32)
    valid = (within[None, :] < peer_counts[:, None]).reshape(-1)
    source = jnp.where(valid, (starts[:, None] + within[None, :]).reshape(-1), 0)
    outgoing_columns = jnp.where(valid, patch_list[source], width)
    arrived_columns = lax.all_to_all(
        outgoing_columns, "sub", split_axis=0, concat_axis=0, tiled=True
    )
    blocks = tangent(grads, mods, extra)
    outgoing = blocks[:, source] * valid.astype(jnp.float32)[None, :]
    arrived = lax.all_to_all(outgoing, "sub", split_axis=1, concat_axis=1, tiled=True)
    stiff = jnp.zeros((144, width), jnp.float32).at[:, arrived_columns].add(arrived, mode="drop")
    lumped = stiff + jnp.eye(12, dtype=jnp.float32).reshape(144, 1)
    inverse = jnp.zeros((width,), jnp.int32).at[facing].set(jnp.arange(width, dtype=jnp.int32))

    def apply_lumped(vectors):
        return coupled(lumped, vectors, facing, inverse)

    resid = rhs[:, 0, :]
    multipliers = jnp.zeros_like(resid)
    precond = apply_lumped(resid)
    direction = precond
    rz_now = resid_sum(resid, precond)
    for iteration in range(ITERS):
        image = coupled(comp, direction, facing, inverse)
        alpha = rz_now / lax.psum(jnp.sum(direction * image), ("sub", "grp"))
        multipliers = multipliers + alpha * direction
        resid = resid - alpha * image
        if iteration + 1 < ITERS:
            precond = apply_lumped(resid)
            rz_next = resid_sum(resid, precond)
            direction = precond + rz_next / rz_now * direction
            rz_now = rz_next
    return (multipliers[:, None, :], stiff[:, None, :])


def solution(mesh):
    in_specs = (
        P(None, None, "grp", "sub"),
        P(None, "grp", "sub"),
        P(None, "grp", "sub"),
        P("grp", "sub", None),
        P("grp", "sub"),
        P(None, "grp", "sub"),
        P("grp", "sub", None),
        P(None, "grp", "sub"),
    )
    out_specs = (P(None, "grp", "sub"), P(None, "grp", "sub"))
    return jax.shard_map(
        per_device, mesh=mesh, in_specs=in_specs, out_specs=out_specs, check_vma=False
    )
```

profile of v0, /device:TPU:1, one launch (start us, length us, event | category | flops | bytes accessed | tf_op | source)
XLA Modules:
  0.0 447.7 jit_solution(10329864112774198252)
XLA Ops:
  3.3 9.5 %gather_fusion = s32[1536]{0:T(1024)S(1)} fusion(s32[512]{0:T(512)S(1)} %bitcast.141, s32[2048]{0:T(1024)S(1)} %pad_clamp_fusion), kind=kCustom, calls=%fused_computation | custom fusion | bytes 18432 | tf_op jit(solution)/shard_map/gather | solution.py:59
  13.6 18.4 %all-to-all-start = ((s32[128,12,1]{1,2,0:T(1,128)}), s32[128,12,1]{1,2,0:T(1,128)S(1)}, u32[]{:S(2)}, u32[]{:S(2)}) async-start(s32[128,12,1]{1,2,0:T(1,128)} %bitcast.3), calls=%async_computation | async-start | bytes 131072 | tf_op jit(solution)/shard_map/all_to_all | solution.py:60
  33.3 4.7 %gather_fusion.1 = f32[1536,144]{1,0:T(8,128)} fusion(f32[144,512]{0,1:T(8,128)S(1)} %copy.78, s32[2048]{0:T(1024)S(1)} %pad_clamp_fusion), kind=kCustom, calls=%fused_computation.1 | custom fusion | bytes 1775616 | tf_op jit(solution)/shard_map/gather | solution.py:64
  41.2 4.1 reshape.605
  45.2 13.9 %all-to-all-start.1 = ((f32[128,1,1728]{2,1,0:T(1,128)}), f32[128,1,1728]{2,1,0:T(1,128)S(1)}, u32[]{:S(2)}, u32[]{:S(2)}) async-start(f32[128,1,1728]{2,1,0:T(1,128)} %reshape.605), calls=%async_computation.1 | async-start | bytes 1835008 | tf_op jit(solution)/shard_map/all_to_all | solution.py:65
  60.9 3.3 collective-permute-start
  64.2 3.2 collective-permute-done
  69.0 18.0 %all-to-all-done.1 = f32[128,1,1728]{2,1,0:T(1,128)S(1)} async-done(((f32[128,1,1728]{2,1,0:T(1,128)}), f32[128,1,1728]{2,1,0:T(1,128)S(1)}, u32[]{:S(2)}, u32[]{:S(2)}) %all-to-all-start.1) | async-done | bytes 884768 | tf_op jit(solution)/shard_map/all_to_all | solution.py:65
  87.5 2.8 reduce.13
  93.1 9.4 %scatter_custom_fusion = f32[144,128]{0,1:T(8,128)S(1)} fusion(s32[1536]{0:T(1024)S(1)} %fusion.18, f32[144,1536]{0,1:T(8,128)} %reshape.560, f32[]{:T(128)} %constant.4.clone.1), kind=kCustom, calls=%fused_computation.12 | custom fusion | flops 221184 | bytes 958468 | tf_op jit(solution)/shard_map/scatter-add | solution.py:66
  102.8 4.4 collective-permute-start.1
  110.0 2.4 collective-permute-start.2
  113.8 2.8 collective-permute-done.2
  116.8 3.4 collective-permute-start.3
  123.2 99.4 %all-reduce = (f32[]{:T(128)}, f32[]{:T(128)}) all-reduce(f32[]{:T(128)} %get-tuple-element.19, f32[]{:T(128)} %get-tuple-element.18), channel_id=1, replica_groups=mesh['sub'=128,'grp'=4] {'sub','grp'}, use_global_device_ids=true, to_apply=%region_6.7 | all-reduce | flops 2 | bytes 16 | tf_op jit(solution)/shard_map/psum | solution.py:39
  224.6 1.9 collective-permute-start.4
  226.6 4.3 collective-permute-done.4
  233.0 3.1 collective-permute-done.5
  237.4 96.5 %psum.30 = f32[]{:T(128)} all-reduce(f32[]{:T(128)} %multiply_reduce_fusion.8), channel_id=1, replica_groups=mesh['sub'=128,'grp'=4] {'sub','grp'}, use_global_device_ids=true, to_apply=%region_14.15 | all-reduce | flops 1 | bytes 8 | tf_op jit(solution)/shard_map/psum | solution.py:39
  336.1 3.6 collective-permute-start.6
  339.7 2.6 collective-permute-done.6
  342.5 2.4 collective-permute-start.7
  344.9 2.6 collective-permute-done.7
  349.7 96.0 %psum.31 = f32[]{:T(128)} all-reduce(f32[]{:T(128)} %fusion.15), channel_id=1, replica_groups=mesh['sub'=128,'grp'=4] {'sub','grp'}, use_global_device_ids=true, to_apply=%region_18.19 | all-reduce | flops 1 | bytes 8 | tf_op jit(solution)/shard_map/psum | solution.py:80
  (103 shorter events, 29.9 us)
Async XLA Ops:
  0.6 2.6 copy-start
  3.3 9.6 %copy-start.6 = (s32[1,1,128]{2,1,0:T(1,128)S(1)}, s32[1,1,128]{2,1,0:T(1,128)}, u32[]{:S(2)}) copy-start(s32[1,1,128]{2,1,0:T(1,128)} %param.11) | copy-start | bytes 1540
  3.3 28.9 %copy-start.4 = (bf16[9,1,512]{2,0,1:T(8,128)(2,1)S(1)}, bf16[9,1,512]{2,0,1:T(8,128)(2,1)}, u32[]{:S(2)}) copy-start(bf16[9,1,512]{2,0,1:T(8,128)(2,1)} %param.9) | copy-start | bytes 27652
  3.3 28.9 %copy-start.1 = (bf16[9,12,1,512]{3,1,2,0:T(8,128)(2,1)S(1)}, bf16[9,12,1,512]{3,1,2,0:T(8,128)(2,1)}, u32[]{:S(2)}) copy-start(bf16[9,12,1,512]{3,1,2,0:T(8,128)(2,1)} %param.8) | copy-start | bytes 331780
  13.6 31.6 %all-to-all-start = ((s32[128,12,1]{1,2,0:T(1,128)}), s32[128,12,1]{1,2,0:T(1,128)S(1)}, u32[]{:S(2)}, u32[]{:S(2)}) async-start(s32[128,12,1]{1,2,0:T(1,128)} %bitcast.3), calls=%async_computation | async-start | bytes 131072 | tf_op jit(solution)/shard_map/all_to_all | solution.py:60
  32.2 0.7 copy-start.5
  45.2 13.9 %copy-start.2 = (f32[12,1,128]{2,1,0:T(1,128)S(1)}, f32[12,1,128]{2,1,0:T(1,128)}, u32[]{:S(2)}) copy-start(f32[12,1,128]{2,1,0:T(1,128)} %param.15) | copy-start | bytes 18436
  45.2 14.0 %copy-start.7 = (s32[1,1,128]{2,1,0:T(1,128)S(1)}, s32[1,1,128]{2,1,0:T(1,128)}, u32[]{:S(2)}) copy-start(s32[1,1,128]{2,1,0:T(1,128)} %param.14) | copy-start | bytes 1540
  45.2 41.7 %all-to-all-start.1 = ((f32[128,1,1728]{2,1,0:T(1,128)}), f32[128,1,1728]{2,1,0:T(1,128)S(1)}, u32[]{:S(2)}, u32[]{:S(2)}) async-start(f32[128,1,1728]{2,1,0:T(1,128)} %reshape.605), calls=%async_computation.1 | async-start | bytes 1835008 | tf_op jit(solution)/shard_map/all_to_all | solution.py:65
  60.9 6.5 %collective-permute-start = (f32[12,128]{0,1:T(8,128)S(1)}, f32[12,128]{0,1:T(8,128)S(1)}, u32[]{:S(2)}, u32[]{:S(2)}) collective-permute-start(f32[12,128]{0,1:T(8,128)S(1)} %bitcast.161), channel_id=1, source_target_pairs={{3,0},{0,1},{1,2},{2,3},{7,4},{4,5},{5,6},{6,7},{11,8},{8,9},{9,10... | collective-permute-start | bytes 18440 | tf_op jit(solution)/shard_map/ppermute | solution.py:12
  93.0 19.9 %copy-start.3 = (f32[144,1,128]{2,1,0:T(1,128)S(1)}, f32[144,1,128]{2,1,0:T(1,128)}, u32[]{:S(2)}) copy-start(f32[144,1,128]{2,1,0:T(1,128)} %param.13) | copy-start | bytes 221188
  102.8 5.7 %collective-permute-start.1 = (f32[12,128]{0,1:T(8,128)S(1)}, f32[12,128]{0,1:T(8,128)S(1)}, u32[]{:S(2)}, u32[]{:S(2)}) collective-permute-start(f32[12,128]{0,1:T(8,128)S(1)} %copy.82), channel_id=1, source_target_pairs={{1,0},{2,1},{3,2},{0,3},{5,4},{6,5},{7,6},{4,7},{9,8},{10,9},{11,1... | collective-permute-start | bytes 18440 | tf_op jit(solution)/shard_map/ppermute | solution.py:12
  110.0 6.5 %collective-permute-start.2 = (f32[12,128]{0,1:T(8,128)S(1)}, f32[12,128]{0,1:T(8,128)S(1)}, u32[]{:S(2)}, u32[]{:S(2)}) collective-permute-start(f32[12,128]{0,1:T(8,128)S(1)} %bitcast.160), channel_id=1, source_target_pairs={{3,0},{0,1},{1,2},{2,3},{7,4},{4,5},{5,6},{6,7},{11,8},{8,9},{9,10... | collective-permute-start | bytes 18440 | tf_op jit(solution)/shard_map/ppermute | solution.py:12
  116.8 5.0 %collective-permute-start.3 = (f32[12,128]{0,1:T(8,128)S(1)}, f32[12,128]{0,1:T(8,128)S(1)}, u32[]{:S(2)}, u32[]{:S(2)}) collective-permute-start(f32[12,128]{0,1:T(8,128)S(1)} %copy.86), channel_id=1, source_target_pairs={{1,0},{2,1},{3,2},{0,3},{5,4},{6,5},{7,6},{4,7},{9,8},{10,9},{11,1... | collective-permute-start | bytes 18440 | tf_op jit(solution)/shard_map/ppermute | solution.py:12
  224.6 6.2 %collective-permute-start.4 = (f32[12,128]{0,1:T(8,128)S(1)}, f32[12,128]{0,1:T(8,128)S(1)}, u32[]{:S(2)}, u32[]{:S(2)}) collective-permute-start(f32[12,128]{0,1:T(8,128)S(1)} %bitcast.163), channel_id=1, source_target_pairs={{3,0},{0,1},{1,2},{2,3},{7,4},{4,5},{5,6},{6,7},{11,8},{8,9},{9,10... | collective-permute-start | bytes 18440 | tf_op jit(solution)/shard_map/ppermute | solution.py:12
  231.1 5.0 %collective-permute-start.5 = (f32[12,128]{0,1:T(8,128)S(1)}, f32[12,128]{0,1:T(8,128)S(1)}, u32[]{:S(2)}, u32[]{:S(2)}) collective-permute-start(f32[12,128]{0,1:T(8,128)S(1)} %copy.90), channel_id=1, source_target_pairs={{1,0},{2,1},{3,2},{0,3},{5,4},{6,5},{7,6},{4,7},{9,8},{10,9},{11,1... | collective-permute-start | bytes 18440 | tf_op jit(solution)/shard_map/ppermute | solution.py:12
  336.1 6.2 %collective-permute-start.6 = (f32[12,128]{0,1:T(8,128)S(1)}, f32[12,128]{0,1:T(8,128)S(1)}, u32[]{:S(2)}, u32[]{:S(2)}) collective-permute-start(f32[12,128]{0,1:T(8,128)S(1)} %bitcast.162), channel_id=1, source_target_pairs={{3,0},{0,1},{1,2},{2,3},{7,4},{4,5},{5,6},{6,7},{11,8},{8,9},{9,10... | collective-permute-start | bytes 18440 | tf_op jit(solution)/shard_map/ppermute | solution.py:12
  342.5 5.0 %collective-permute-start.7 = (f32[12,128]{0,1:T(8,128)S(1)}, f32[12,128]{0,1:T(8,128)S(1)}, u32[]{:S(2)}, u32[]{:S(2)}) collective-permute-start(f32[12,128]{0,1:T(8,128)S(1)} %copy.94), channel_id=1, source_target_pairs={{1,0},{2,1},{3,2},{0,3},{5,4},{6,5},{7,6},{4,7},{9,8},{10,9},{11,1... | collective-permute-start | bytes 18440 | tf_op jit(solution)/shard_map/ppermute | solution.py:12
where the time goes:
time: 449 us; the launch traced here: 448 us
  blocking collectives  292 us (65%)
  starting transfers between devices  55.5 us (12%)
  waiting for transfers between devices  39.6 us (9%)
  local copies, waits for them, and re-layouts  34.7 us (8%)
  other arithmetic  20.9 us (5%)
  between operations  5.21 us (1%)
    psum x2, blocking collectives, resid_sum(): return lax.psum(jnp.sum(resid * precond), ('sub', 'grp'))  196 us
    psum x1, blocking collectives, per_device(): alpha = rz_now / lax.psum(jnp.sum(direction * image), ('sub', 'grp'))  96 us
    ppermute x8, starting transfers between devices, from_behind(): return lax.ppermute(block, axis, route)  23.2 us
    ppermute x8, waiting for transfers between devices, from_behind(): return lax.ppermute(block, axis, route)  21.5 us
    all_to_all x1, starting transfers between devices, per_device(): lax.all_to_all(outgoing_columns, 'sub', split_axis=0, concat_axis=0, tile...  18.4 us
    all_to_all x1, waiting for transfers between devices, per_device(): lax.all_to_all(outgoing, 'sub', split_axis=1, concat_axis=1, tiled=True)  18 us
    all_to_all x1, starting transfers between devices, per_device(): lax.all_to_all(outgoing, 'sub', split_axis=1, concat_axis=1, tiled=True)  13.9 us
    gather x2, local copies, waits for them, and re-layouts, per_device(): outgoing_columns = jnp.where(valid, patch_list[source], width)  9.57 us
  transfers between devices with their start and end apart: 10, of which 9 were waited for; matrix products, arithmetic and copies ran while one was open for 4% of the time, Pallas kernels for 0%

commit v1 on v0

v1 whole, which is shorter than its diff:
```python
import jax
import jax.numpy as jnp
from jax import lax
from jax.experimental import pallas as pl
from jax.experimental.pallas import tpu as pltpu
from jax.sharding import PartitionSpec as P

MESH = pl.DeviceIdType.MESH
F32, BF16, I32 = jnp.float32, jnp.bfloat16, jnp.int32
N = 12
HALF = 7
ROW, COL, GRP = 16, 8, 4
SUB = ROW * COL
ELEMS = 512
COLS = 128
CAP = 12
WORDS = 42
LANES_OF = 3
ROWS_OF = CAP // LANES_OF
SLOT_ROWS = SUB * ROWS_OF


def dot_nt(a, b):
    return lax.dot_general(a, b, (((1,), (1,)), ((), ())), preferred_element_type=F32)


def tangents(grads, mods, diag):
    sums = [None] * HALF
    for m in range(9):
        g = grads[m]
        weighted = g * mods[m : m + 1]
        wrapped = jnp.concatenate([g, g[:6]], axis=0)
        for d in range(HALF):
            rows = 6 if d == 6 else N
            term = weighted[:rows] * wrapped[d : d + rows]
            sums[d] = term if sums[d] is None else sums[d] + term
    sums[0] = sums[0] + diag
    return sums


def apply_half(k, v):
    twice = jnp.concatenate([v, v], axis=0)
    out = k[0] * v
    for d in range(1, 6):
        out = out + k[d] * twice[d : d + N]
        back = k[d] * v
        back = jnp.concatenate([back, back], axis=0)
        out = out + back[N - d : 2 * N - d]
    k6 = jnp.concatenate([k[6], k[6]], axis=0)
    return out + k6 * twice[6 : 6 + N]


def apply_full(k_ref, v):
    out = None
    for b in range(N):
        term = k_ref[b * N : (b + 1) * N, :] * v[b : b + 1]
        out = term if out is None else out + term
    return out


def combine(slots, count):
    row = lax.broadcasted_iota(I32, (8, COLS), 0)
    top = slots[0, 4:5]
    for i in range(1, count):
        top = jnp.maximum(top, slots[i, 4:5])
    total = None
    for i in range(count):
        term = weigh(slots[i], slots[i, 4:5] / top, row)
        total = term if total is None else total + term
    return jnp.where(row == 4, jnp.broadcast_to(top, (8, COLS)), total)


def weigh(block, ratio, row):
    ratio = jnp.broadcast_to(ratio, (8, COLS))
    square = ratio * ratio
    factor = jnp.where(row == 1, ratio, jnp.where(row == 2, square, square * ratio))
    return block * jnp.where(row == 0, 1.0, factor)


def kernel(
    grads, mods, diag, counts, targets, comp, neigh, rhs,
    lam_out, stiff_out,
    g_v, m_v, d_v, c_v, t_v, n_v, r_v, own_c, near_c,
    sel, rhs_h, rhs_l, send, recv, half_own, half_near, stiff_v, lam_v,
    mine, slots_a, slots_b, slots_c,
    in_sem, row_sem, comp_sems, out_sems, local_sem, move_sems, half_sems, sem_a, sem_b, sem_c,
):
    me, grp = lax.axis_index("sub"), lax.axis_index("grp")
    y, zc = me // ROW, me % ROW
    behind = (me, (grp + GRP - 1) % GRP)

    barrier = pltpu.get_barrier_semaphore()

    def greet(device):
        pl.semaphore_signal(barrier, inc=1, device_id=device, device_id_type=MESH)

    for d in range(1, COL):
        greet((((y + d) % COL) * ROW + zc, grp))
    for d in range(1, ROW):
        greet((y * ROW + (zc + d) % ROW, grp))
    for d in range(1, GRP):
        greet((me, (grp + d) % GRP))

    loads = [(grads, g_v), (mods, m_v), (diag, d_v), (counts, c_v), (targets, t_v),
             (neigh, n_v), (rhs, r_v), (comp, own_c)]
    loads = [pltpu.make_async_copy(a, b, in_sem.at[i]) for i, (a, b) in enumerate(loads)]
    for copy in loads:
        copy.start()
    for copy in loads[:5]:
        copy.wait()

    mods_f = m_v[...].astype(F32)
    for t in range(ELEMS // COLS):
        at = pl.ds(t * COLS, COLS)
        tile = tangents(
            [g_v[m, :, at].astype(F32) for m in range(9)],
            mods_f[:, t * COLS : (t + 1) * COLS],
            d_v[:, at].astype(F32),
        )
        biggest = jnp.max(tile[0], axis=0, keepdims=True)
        step = (biggest * 1.01).astype(BF16).astype(F32)
        scale = 32768.0 / step
        meta = jnp.concatenate(
            [t_v[:, at].astype(F32), step * 512.0, jnp.zeros((4, COLS), F32)], axis=0
        )
        high = [jnp.floor(tile[d] * scale + 0.5) for d in (0, 2, 4, 6)]
        low = [jnp.floor(tile[d] * scale + 0.5) for d in (1, 3, 5)] + [meta]
        for half, values in enumerate((high, low)):
            values = jnp.concatenate(values, axis=0)
            upper = jnp.floor(values * (1.0 / 256.0)) * 256.0
            for piece, ref in ((upper, rhs_h), (values - upper, rhs_l)):
                for j in range(LANES_OF):
                    parts = [piece]
                    if j:
                        parts = [jnp.zeros((j * WORDS, COLS), F32)] + parts
                    parts = parts + [jnp.zeros((COLS - (j + 1) * WORDS, COLS), F32)]
                    ref[half * COLS : (half + 1) * COLS, pl.ds(j * ELEMS + t * COLS, COLS)] = (
                        jnp.concatenate(parts, axis=0).astype(BF16)
                    )

    line = lax.broadcasted_iota(I32, (SLOT_ROWS, COLS), 0)
    lane = lax.broadcasted_iota(I32, (SLOT_ROWS, COLS), 1)
    per_peer = jnp.broadcast_to(c_v[...].astype(F32), (COLS, SUB)).astype(BF16)
    first = dot_nt((lane < line // ROWS_OF).astype(F32).astype(BF16), per_peer)
    listed = dot_nt((lane == line // ROWS_OF).astype(F32).astype(BF16), per_peer)
    place = ((line % ROWS_OF) * LANES_OF).astype(F32)
    lane_f = lane.astype(F32)
    for j in range(LANES_OF):
        wanted = jnp.where(place + j < listed, first + place + j, -1.0)
        for t in range(ELEMS // COLS):
            hit = jnp.where(wanted == lane_f + t * COLS, 1.0, 0.0)
            sel[:, pl.ds(j * ELEMS + t * COLS, COLS)] = hit.astype(BF16)

    pl.semaphore_wait(barrier, ROW + COL + GRP - 3)
    for d in range(1, COL):
        pl.semaphore_signal(
            row_sem, inc=1, device_id=(((y + d) % COL) * ROW + zc, grp), device_id_type=MESH
        )
    for copy in loads[5:]:
        copy.wait()
    comp_copy = pltpu.make_async_remote_copy(
        own_c, near_c, comp_sems.at[0], comp_sems.at[1], device_id=behind, device_id_type=MESH
    )
    comp_copy.start()

    for c in range(4):
        rows = pl.ds(c * 128, 128)
        packed = dot_nt(sel[rows, :], rhs_h[...]) + dot_nt(sel[rows, :], rhs_l[...])
        packed = packed.astype(I32)
        words = (packed[:, :COLS] << 16) | (packed[:, COLS:] & 0xFFFF)
        send[pl.ds(c * 32, 32)] = words.reshape(32, ROWS_OF, COLS)

    pl.semaphore_wait(row_sem, COL - 1)
    local = pltpu.make_async_copy(send.at[me], recv.at[me], local_sem)
    local.start()

    @pl.loop(1, SUB)
    def _(d):
        peer = me ^ d
        pltpu.make_async_remote_copy(
            send.at[peer], recv.at[me], move_sems.at[0], move_sems.at[1],
            device_id=(peer, grp), device_id_type=MESH,
        ).start()

    comp_copy.wait()
    facing = jnp.broadcast_to(n_v[...], (8, COLS))

    def moved(block):
        rows = block.shape[0]
        if rows % 8:
            block = jnp.concatenate([block, jnp.zeros((8 - rows % 8, COLS), F32)], axis=0)
        parts = [
            jnp.take_along_axis(block[i : i + 8], facing, axis=1)
            for i in range(0, block.shape[0], 8)
        ]
        return jnp.concatenate(parts, axis=0)[:rows]

    both_c = own_c[...] + moved(near_c[...])
    unit = both_c[0:1]
    for a in range(1, N):
        unit = jnp.maximum(unit, both_c[a * (N + 1) : a * (N + 1) + 1])
    own_c[...] = both_c / unit

    local.wait()
    others = recv.at[pl.ds(0, SUB - 1)]
    pltpu.make_async_copy(others, others, move_sems.at[1]).wait()

    words = recv[...].reshape(SLOT_ROWS, COLS)
    high = words >> 16
    low = (words << 16) >> 16
    pieces = [high >> 8, high & 255, low >> 8, low & 255]
    pieces = jnp.concatenate([p.astype(F32).astype(BF16) for p in pieces], axis=1)
    meta = low.astype(F32).T
    patch = lax.broadcasted_iota(I32, (COLS, SLOT_ROWS), 0).astype(F32)
    lane = lax.broadcasted_iota(I32, (COLS, COLS), 1)
    sums = [jnp.zeros((COLS, COLS), F32)] * 2
    for j in range(LANES_OF):
        target = meta[j * WORDS + 36 : j * WORDS + 37]
        code = meta[j * WORDS + 37 : j * WORDS + 38]
        step = jnp.where(code < 0.0, code + 65536.0, code) * (1.0 / 512.0)
        hit = jnp.where(patch == target, step, 0.0).astype(BF16)
        part = jnp.dot(hit, pieces, preferred_element_type=F32)
        here = (lane >= j * WORDS) & (lane < (j + 1) * WORDS)
        for half in range(2):
            upper = part[:, half * 256 : half * 256 + 128]
            lower = part[:, half * 256 + 128 : half * 256 + 256]
            sums[half] = sums[half] + jnp.where(here, upper * 256.0 + lower, 0.0)
    for half in range(2):
        turned = sums[half].T * (1.0 / 32768.0)
        folded = turned[:WORDS] + turned[WORDS : 2 * WORDS] + turned[2 * WORDS : 3 * WORDS]
        half_own[half * 48 : half * 48 + 48, :] = jnp.concatenate(
            [folded, jnp.zeros((6, COLS), F32)], axis=0
        )
    half_copy = pltpu.make_async_remote_copy(
        half_own, half_near, half_sems.at[0], half_sems.at[1], device_id=behind, device_id_type=MESH
    )
    half_copy.start()
    start_of = [0, 48, 12, 60, 24, 72, 36]
    for a in range(N):
        for b in range(N):
            d = (b - a) % N
            source = start_of[d] + a % (6 if d == 6 else N) if d < HALF else start_of[N - d] + b
            stiff_v[a * N + b : a * N + b + 1, :] = half_own[source : source + 1, :]
    stiff_copy = pltpu.make_async_copy(stiff_v, stiff_out, out_sems.at[0])
    stiff_copy.start()
    half_copy.wait()

    both = half_own[...] + moved(half_near[...])
    k = [both[s : s + (6 if d == 6 else N)] for d, s in enumerate(start_of)]
    k[0] = k[0] + 2.0

    resid = r_v[...]
    precond = apply_half(k, resid)
    image = apply_full(own_c, precond)
    again = apply_half(k, image)
    image_again = apply_full(own_c, again)

    def inner(a, b):
        return jnp.sum(a * b, axis=0, keepdims=True)

    mine[...] = jnp.concatenate(
        [inner(resid, precond), inner(precond, image), inner(image, again),
         inner(again, image_again), unit, jnp.zeros((3, COLS), F32)], axis=0,
    )

    def spread(slots, count, here, device_of, sems):
        slots[here] = mine[...]
        for d in range(1, count):
            pltpu.make_async_remote_copy(
                mine, slots.at[here], sems.at[0], sems.at[1],
                device_id=device_of((here + d) % count), device_id_type=MESH,
            ).start()
        rest = slots.at[pl.ds(0, count - 1)]
        pltpu.make_async_copy(rest, rest, sems.at[1]).wait()
        pltpu.make_async_copy(rest, rest, sems.at[0]).wait()
        mine[...] = combine(slots, count)

    spread(slots_a, ROW, zc, lambda i: (y * ROW + i, grp), sem_a)
    spread(slots_b, COL, y, lambda i: (i * ROW + zc, grp), sem_b)
    spread(slots_c, GRP, grp, lambda i: (me, i), sem_c)

    total = mine[...]
    row = lax.broadcasted_iota(I32, (8, COLS), 0)
    top = jnp.max(total[4:5], axis=1, keepdims=True)
    total = jnp.sum(weigh(total, total[4:5] / top, row), axis=1, keepdims=True)
    rz, pq, quq, uw = (total[i : i + 1] for i in range(4))
    alpha = rz / pq
    rz_next = alpha * alpha * quq - rz
    grown = 1.0 + rz_next / rz
    alpha_next = rz_next / (alpha * alpha * uw - grown * grown * pq)
    lam_v[...] = (
        (alpha + alpha_next * grown) / top * precond
        - alpha_next * alpha / top * (unit / top) * again
    )
    lam_copy = pltpu.make_async_copy(lam_v, lam_out, out_sems.at[1])
    lam_copy.start()
    pltpu.make_async_copy(others, others, move_sems.at[0]).wait()
    stiff_copy.wait()
    lam_copy.wait()


def per_device(gradients, moduli, diag_terms, counts, targets, compliance, neighbours, rhs):
    vmem = lambda shape, dtype=F32: pltpu.VMEM(shape, dtype)
    dma = pltpu.SemaphoreType.DMA
    lam, stiff = pl.pallas_call(
        kernel,
        out_shape=(
            jax.ShapeDtypeStruct((N, COLS), F32),
            jax.ShapeDtypeStruct((N * N, COLS), F32),
        ),
        in_specs=[pl.BlockSpec(memory_space=pl.ANY)] * 8,
        out_specs=[pl.BlockSpec(memory_space=pl.ANY)] * 2,
        scratch_shapes=[
            vmem((9, N, ELEMS), BF16),
            vmem((9, ELEMS), BF16),
            vmem((N, ELEMS), BF16),
            vmem((1, SUB), I32),
            vmem((1, ELEMS), I32),
            vmem((1, COLS), I32),
            vmem((N, COLS)),
            vmem((N * N, COLS)),
            vmem((N * N, COLS)),
            vmem((SLOT_ROWS, LANES_OF * ELEMS), BF16),
            vmem((2 * COLS, LANES_OF * ELEMS), BF16),
            vmem((2 * COLS, LANES_OF * ELEMS), BF16),
            vmem((SUB, ROWS_OF, COLS), I32),
            vmem((SUB, ROWS_OF, COLS), I32),
            vmem((96, COLS)),
            vmem((96, COLS)),
            vmem((N * N, COLS)),
            vmem((N, COLS)),
            vmem((8, COLS)),
            vmem((ROW, 8, COLS)),
            vmem((COL, 8, COLS)),
            vmem((GRP, 8, COLS)),
            dma((8,)),
            pltpu.SemaphoreType.REGULAR,
            dma((2,)),
            dma((2,)),
            dma,
            dma((2,)),
            dma((2,)),
            dma((2,)),
            dma((2,)),
            dma((2,)),
        ],
        compiler_params=pltpu.CompilerParams(
            collective_id=0, has_side_effects=True, vmem_limit_bytes=32 * 1024 * 1024
        ),
    )(
        gradients[:, :, 0, :],
        moduli[:, 0, :],
        diag_terms[:, 0, :],
        counts[0],
        targets,
        compliance[:, 0, :],
        neighbours[0],
        rhs[:, 0, :],
    )
    return lam[:, None, :], stiff[:, None, :]


def solution(mesh):
    in_specs = (
        P(None, None, "grp", "sub"),
        P(None, "grp", "sub"),
        P(None, "grp", "sub"),
        P("grp", "sub", None),
        P("grp", "sub"),
        P(None, "grp", "sub"),
        P("grp", "sub", None),
        P(None, "grp", "sub"),
    )
    out_specs = (P(None, "grp", "sub"), P(None, "grp", "sub"))
    return jax.shard_map(
        per_device, mesh=mesh, in_specs=in_specs, out_specs=out_specs, check_vma=False
    )
```

time: 449 us -> 52 us (0.12)
  blocking collectives: 292 us -> 0 us
  starting transfers between devices: 55.5 us -> 0 us
  Pallas kernels: 0 us -> 46 us
  waiting for transfers between devices: 39.6 us -> 0 us
  local copies, waits for them, and re-layouts: 34.7 us -> 5.1 us
  other arithmetic: 20.9 us -> 0 us
  between operations: 5.21 us -> 0.67 us
    psum x3 -> x0, blocking collectives: 292 us -> none  [the longest x2 196 us: resid_sum(): return lax.psum(jnp.sum(resid * precond), ('sub', 'grp'))]
    pallas_call x0 -> x1, Pallas kernels: none -> 46 us  [per_device(): pl.pallas_call(kernel, out_shape=(jax.ShapeDtypeStruct((N, COLS), F32), j...]
    all_to_all x2 -> x0, starting transfers between devices: 32.3 us -> none  [the longest x1 18.4 us: per_device(): lax.all_to_all(outgoing_columns, 'sub', split_axis=0, concat_axis=0, tile...]
    ppermute x8 -> x0, starting transfers between devices: 23.2 us -> none  [from_behind(): return lax.ppermute(block, axis, route)]
    ppermute x8 -> x0, waiting for transfers between devices: 21.5 us -> none  [from_behind(): return lax.ppermute(block, axis, route)]
    gather x16 -> x0, local copies, waits for them, and re-layouts: 21.1 us -> none  [the longest x2 9.57 us: per_device(): outgoing_columns = jnp.where(valid, patch_list[source], width)]
    all_to_all x2 -> x0, waiting for transfers between devices: 18 us -> none  [the longest x1 18 us: per_device(): lax.all_to_all(outgoing, 'sub', split_axis=1, concat_axis=1, tiled=True)]
    scatter-add x1 -> x0, other arithmetic: 9.41 us -> none  [per_device(): jnp.zeros((144, width), jnp.float32).at[:, arrived_columns]]
  transfers between devices with their start and end apart: 10 -> 0, of which waited for: 9 -> 0; matrix products, arithmetic and copies ran while one was open for 4% -> 0% of each run, Pallas kernels for 0% -> 0%
where the time goes in v1:
time: 52 us; the launch traced here: 51.7 us
  Pallas kernels  46 us (88%)
  local copies, waits for them, and re-layouts  5.1 us (10%)
  between operations  0.67 us (1%)
    pallas_call x1, Pallas kernels, per_device(): pl.pallas_call(kernel, out_shape=(jax.ShapeDtypeStruct((N, COLS), F32), j...  46 us
    unnamed x19, local copies, waits for them, and re-layouts  5.1 us

profile of v1, /device:TPU:1, one launch (start us, length us, event | category | flops | bytes accessed | tf_op | source)
XLA Modules:
  0.0 51.7 jit_solution(1114280768105084931)
XLA Ops:
  0.6 0.0 copy-start.7
  0.6 0.0 copy-start.2
  0.7 0.7 %copy-done.7 = f32[12,1,128]{2,1,0:T(1,128)S(1)} copy-done((f32[12,1,128]{2,1,0:T(1,128)S(1)}, f32[12,1,128]{2,1,0:T(1,128)}, u32[]{:S(2)}) %copy-start.7) | copy-done | bytes 6168
  1.3 0.0 copy-start.4
  1.3 0.0 copy-start.5
  1.3 0.0 copy-start.6
  1.3 0.0 copy-done.2
  1.4 0.6 %copy-done.4 = s32[1,512]{1,0:T(1,128)S(1)} copy-done((s32[1,512]{1,0:T(1,128)S(1)}, s32[1,512]{1,0:T(1,128)}, u32[]{:S(2)}) %copy-start.4) | copy-done | bytes 2072
  2.0 0.0 copy-done.5
  2.0 0.0 copy-done.6
  2.0 0.0 copy-start
  2.0 0.9 %copy-done = bf16[9,12,1,512]{3,1,2,0:T(8,128)(2,1)S(1)} copy-done((bf16[9,12,1,512]{3,1,2,0:T(8,128)(2,1)S(1)}, bf16[9,12,1,512]{3,1,2,0:T(8,128)(2,1)}, u32[]{:S(2)}) %copy-start) | copy-done | bytes 110616
  2.9 0.0 copy-start.1
  2.9 0.9 %copy-done.1 = f32[144,1,128]{2,1,0:T(1,128)S(1)} copy-done((f32[144,1,128]{2,1,0:T(1,128)S(1)}, f32[144,1,128]{2,1,0:T(1,128)}, u32[]{:S(2)}) %copy-start.1) | copy-done | bytes 73752
  3.8 0.0 copy-start.3
  3.8 0.7 %copy-done.3 = bf16[12,1,512]{2,0,1:T(8,128)(2,1)S(1)} copy-done((bf16[12,1,512]{2,0,1:T(8,128)(2,1)S(1)}, bf16[12,1,512]{2,0,1:T(8,128)(2,1)}, u32[]{:S(2)}) %copy-start.3) | copy-done | bytes 12312
  4.5 46.0 %shard_map.95 = (f32[12,128]{1,0:T(8,128)S(1)}, f32[144,128]{1,0:T(8,128)S(1)}) custom-call(bf16[9,12,512]{2,1,0:T(8,128)(2,1)S(1)} %bitcast.13, bf16[9,512]{1,0:T(8,128)(2,1)S(1)} %bitcast.17, bf16[12,512]{1,0:T(8,128)(2,1)S(1)} %bitcast.18, s32[1,128]{1,0:T(1,128)S(1)} %bitcast.20, s32[1,512]{1,0:T(1,128)S(1)} %copy-done.4, f32[144,128]{1,0:T(8,128)S(1)} %bitcast.15, ...), custom_call_target="tpu_custom_call" | custom-call | tf_op jit(solution)/shard_map/pallas_call | solution.py:305
  50.5 0.6 %copy.10 = f32[12,1,128]{2,1,0:T(1,128)} copy(f32[12,1,128]{2,0,1:T(8,128)S(1)} %bitcast.19) | data formatting | bytes 12288
  51.1 0.6 %copy.16 = f32[144,1,128]{2,1,0:T(1,128)} copy(f32[144,1,128]{2,1,0:T(1,128)S(1)} %bitcast.14) | data formatting | bytes 147456
  (1 shorter events, 0.0 us)
Async XLA Ops:
  0.6 0.7 %copy-start.7 = (f32[12,1,128]{2,1,0:T(1,128)S(1)}, f32[12,1,128]{2,1,0:T(1,128)}, u32[]{:S(2)}) copy-start(f32[12,1,128]{2,1,0:T(1,128)} %param.15) | copy-start | bytes 18436
  0.6 0.7 %copy-start.2 = (bf16[9,1,512]{2,0,1:T(8,128)(2,1)S(1)}, bf16[9,1,512]{2,0,1:T(8,128)(2,1)}, u32[]{:S(2)}) copy-start(bf16[9,1,512]{2,0,1:T(8,128)(2,1)} %param.9) | copy-start | bytes 27652
  1.3 0.7 %copy-start.4 = (s32[1,512]{1,0:T(1,128)S(1)}, s32[1,512]{1,0:T(1,128)}, u32[]{:S(2)}) copy-start(s32[1,512]{1,0:T(1,128)} %targets.1) | copy-start | bytes 6148
  1.3 0.7 %copy-start.5 = (s32[1,1,128]{2,1,0:T(1,128)S(1)}, s32[1,1,128]{2,1,0:T(1,128)}, u32[]{:S(2)}) copy-start(s32[1,1,128]{2,1,0:T(1,128)} %param.11) | copy-start | bytes 1540
  1.3 0.7 %copy-start.6 = (s32[1,1,128]{2,1,0:T(1,128)S(1)}, s32[1,1,128]{2,1,0:T(1,128)}, u32[]{:S(2)}) copy-start(s32[1,1,128]{2,1,0:T(1,128)} %param.14) | copy-start | bytes 1540
  2.0 0.9 %copy-start = (bf16[9,12,1,512]{3,1,2,0:T(8,128)(2,1)S(1)}, bf16[9,12,1,512]{3,1,2,0:T(8,128)(2,1)}, u32[]{:S(2)}) copy-start(bf16[9,12,1,512]{3,1,2,0:T(8,128)(2,1)} %param.8) | copy-start | bytes 331780
  2.9 0.9 %copy-start.1 = (f32[144,1,128]{2,1,0:T(1,128)S(1)}, f32[144,1,128]{2,1,0:T(1,128)}, u32[]{:S(2)}) copy-start(f32[144,1,128]{2,1,0:T(1,128)} %param.13) | copy-start | bytes 221188
  3.8 0.7 %copy-start.3 = (bf16[12,1,512]{2,0,1:T(8,128)(2,1)S(1)}, bf16[12,1,512]{2,0,1:T(8,128)(2,1)}, u32[]{:S(2)}) copy-start(bf16[12,1,512]{2,0,1:T(8,128)(2,1)} %param.10) | copy-start | bytes 36868

commit v2 on v1

--- a/solution.py
+++ b/solution.py
@@ -20,6 +20,19 @@
 SLOT_ROWS = SUB * ROWS_OF
 
 
+def hops(step, size):
+    return min(step % size, -step % size)
+
+
+ROW_STEPS = sorted(((z, c) for z in range(8) for c in range(2) if z or c), key=lambda s: -hops(s[0], 8))
+FAN_STEPS = sorted(
+    ((y, x) for y in range(COL) for x in range(GRP) if y or x),
+    key=lambda s: -hops(s[0], COL) - hops(s[1], GRP),
+)
+ROWS_ORDER = list(range(1, COL))
+COL_STEPS = sorted(range(1, COL), key=lambda s: -hops(s, COL))
+
+
 def dot_nt(a, b):
     return lax.dot_general(a, b, (((1,), (1,)), ((), ())), preferred_element_type=F32)
 
@@ -81,25 +94,33 @@
     grads, mods, diag, counts, targets, comp, neigh, rhs,
     lam_out, stiff_out,
     g_v, m_v, d_v, c_v, t_v, n_v, r_v, own_c, near_c,
-    sel, rhs_h, rhs_l, send, recv, half_own, half_near, stiff_v, lam_v,
-    mine, slots_a, slots_b, slots_c,
-    in_sem, row_sem, comp_sems, out_sems, local_sem, move_sems, half_sems, sem_a, sem_b, sem_c,
+    sel, rhs_h, rhs_l, send, recv, half_own, half_near,
+    mine, row_sum, slots_a, slots_b,
+    in_sem, row_sems, comp_sems, local_sem, move_sems, half_sems, sem_a, sem_b,
 ):
     me, grp = lax.axis_index("sub"), lax.axis_index("grp")
     y, zc = me // ROW, me % ROW
     behind = (me, (grp + GRP - 1) % GRP)
 
+    z, core = zc // 2, zc % 2
+
+    def at(dy=0, dz=0, dc=0, dx=0):
+        row = y if dy == 0 else (y + dy) % COL
+        col = z if dz == 0 else (z + dz) % 8
+        side = core if dc == 0 else 1 - core
+        return row * ROW + col * 2 + side, (grp if dx == 0 else (grp + dx) % GRP)
+
     barrier = pltpu.get_barrier_semaphore()
 
     def greet(device):
         pl.semaphore_signal(barrier, inc=1, device_id=device, device_id_type=MESH)
 
-    for d in range(1, COL):
-        greet((((y + d) % COL) * ROW + zc, grp))
-    for d in range(1, ROW):
-        greet((y * ROW + (zc + d) % ROW, grp))
-    for d in range(1, GRP):
-        greet((me, (grp + d) % GRP))
+    for dz, dc in ROW_STEPS:
+        greet(at(dz=dz, dc=dc))
+    for dy in COL_STEPS:
+        greet(at(dy=dy))
+    for dx in range(1, GRP):
+        greet(at(dx=dx))
 
     loads = [(grads, g_v), (mods, m_v), (diag, d_v), (counts, c_v), (targets, t_v),
              (neigh, n_v), (rhs, r_v), (comp, own_c)]
@@ -111,17 +132,17 @@
 
     mods_f = m_v[...].astype(F32)
     for t in range(ELEMS // COLS):
-        at = pl.ds(t * COLS, COLS)
+        here = pl.ds(t * COLS, COLS)
         tile = tangents(
-            [g_v[m, :, at].astype(F32) for m in range(9)],
+            [g_v[m, :, here].astype(F32) for m in range(9)],
             mods_f[:, t * COLS : (t + 1) * COLS],
-            d_v[:, at].astype(F32),
+            d_v[:, here].astype(F32),
         )
         biggest = jnp.max(tile[0], axis=0, keepdims=True)
         step = (biggest * 1.01).astype(BF16).astype(F32)
         scale = 32768.0 / step
         meta = jnp.concatenate(
-            [t_v[:, at].astype(F32), step * 512.0, jnp.zeros((4, COLS), F32)], axis=0
+            [t_v[:, here].astype(F32), step * 512.0, jnp.zeros((4, COLS), F32)], axis=0
         )
         high = [jnp.floor(tile[d] * scale + 0.5) for d in (0, 2, 4, 6)]
         low = [jnp.floor(tile[d] * scale + 0.5) for d in (1, 3, 5)] + [meta]
@@ -152,9 +173,9 @@
             sel[:, pl.ds(j * ELEMS + t * COLS, COLS)] = hit.astype(BF16)
 
     pl.semaphore_wait(barrier, ROW + COL + GRP - 3)
-    for d in range(1, COL):
+    for dy in COL_STEPS:
         pl.semaphore_signal(
-            row_sem, inc=1, device_id=(((y + d) % COL) * ROW + zc, grp), device_id_type=MESH
+            row_sems.at[COL - dy], inc=1, device_id=at(dy=dy), device_id_type=MESH
         )
     for copy in loads[5:]:
         copy.wait()
@@ -170,17 +191,24 @@
         words = (packed[:, :COLS] << 16) | (packed[:, COLS:] & 0xFFFF)
         send[pl.ds(c * 32, 32)] = words.reshape(32, ROWS_OF, COLS)
 
-    pl.semaphore_wait(row_sem, COL - 1)
     local = pltpu.make_async_copy(send.at[me], recv.at[me], local_sem)
     local.start()
 
-    @pl.loop(1, SUB)
-    def _(d):
-        peer = me ^ d
+    def post(dy, dz, dc):
+        device = at(dy, dz, dc)
         pltpu.make_async_remote_copy(
-            send.at[peer], recv.at[me], move_sems.at[0], move_sems.at[1],
-            device_id=(peer, grp), device_id_type=MESH,
+            send.at[device[0]], recv.at[me], move_sems.at[0], move_sems.at[1],
+            device_id=device, device_id_type=MESH,
         ).start()
+
+    for dy in COL_STEPS:
+        post(dy, 0, 0)
+    for dz, dc in ROW_STEPS:
+        post(0, dz, dc)
+    for dy in ROWS_ORDER:
+        pl.semaphore_wait(row_sems.at[dy], 1)
+        for dz, dc in ROW_STEPS:
+            post(dy, dz, dc)
 
     comp_copy.wait()
     facing = jnp.broadcast_to(n_v[...], (8, COLS))
@@ -240,16 +268,14 @@
         for b in range(N):
             d = (b - a) % N
             source = start_of[d] + a % (6 if d == 6 else N) if d < HALF else start_of[N - d] + b
-            stiff_v[a * N + b : a * N + b + 1, :] = half_own[source : source + 1, :]
-    stiff_copy = pltpu.make_async_copy(stiff_v, stiff_out, out_sems.at[0])
-    stiff_copy.start()
+            stiff_out[a * N + b] = half_own[source : source + 1, :]
     half_copy.wait()
 
     both = half_own[...] + moved(half_near[...])
     k = [both[s : s + (6 if d == 6 else N)] for d, s in enumerate(start_of)]
     k[0] = k[0] + 2.0
 
-    resid = r_v[...]
+    resid = r_v[:, 0, :]
     precond = apply_half(k, resid)
     image = apply_full(own_c, precond)
     again = apply_half(k, image)
@@ -263,23 +289,26 @@
          inner(again, image_again), unit, jnp.zeros((3, COLS), F32)], axis=0,
     )
 
-    def spread(slots, count, here, device_of, sems):
-        slots[here] = mine[...]
-        for d in range(1, count):
+    def spread(source, slots, here, steps, sems):
+        count = len(steps) + 1
+        slots[here] = source[...]
+        for step in steps:
             pltpu.make_async_remote_copy(
-                mine, slots.at[here], sems.at[0], sems.at[1],
-                device_id=device_of((here + d) % count), device_id_type=MESH,
+                source, slots.at[here], sems.at[0], sems.at[1],
+                device_id=at(**step), device_id_type=MESH,
             ).start()
         rest = slots.at[pl.ds(0, count - 1)]
         pltpu.make_async_copy(rest, rest, sems.at[1]).wait()
+        return combine(slots, count)
+
+    def sent(slots, steps, sems):
+        rest = slots.at[pl.ds(0, len(steps))]
         pltpu.make_async_copy(rest, rest, sems.at[0]).wait()
-        mine[...] = combine(slots, count)
-
-    spread(slots_a, ROW, zc, lambda i: (y * ROW + i, grp), sem_a)
-    spread(slots_b, COL, y, lambda i: (i * ROW + zc, grp), sem_b)
-    spread(slots_c, GRP, grp, lambda i: (me, i), sem_c)
-
-    total = mine[...]
+
+    row_steps = [dict(dz=dz, dc=dc) for dz, dc in ROW_STEPS]
+    fan_steps = [dict(dy=dy, dx=dx) for dy, dx in FAN_STEPS]
+    row_sum[...] = spread(mine, slots_a, zc, row_steps, sem_a)
+    total = spread(row_sum, slots_b, y * GRP + grp, fan_steps, sem_b)
     row = lax.broadcasted_iota(I32, (8, COLS), 0)
     top = jnp.max(total[4:5], axis=1, keepdims=True)
     total = jnp.sum(weigh(total, total[4:5] / top, row), axis=1, keepdims=True)
@@ -288,15 +317,13 @@
     rz_next = alpha * alpha * quq - rz
     grown = 1.0 + rz_next / rz
     alpha_next = rz_next / (alpha * alpha * uw - grown * grown * pq)
-    lam_v[...] = (
+    lam_out[:, 0, :] = (
         (alpha + alpha_next * grown) / top * precond
         - alpha_next * alpha / top * (unit / top) * again
     )
-    lam_copy = pltpu.make_async_copy(lam_v, lam_out, out_sems.at[1])
-    lam_copy.start()
+    sent(slots_a, row_steps, sem_a)
+    sent(slots_b, fan_steps, sem_b)
     pltpu.make_async_copy(others, others, move_sems.at[0]).wait()
-    stiff_copy.wait()
-    lam_copy.wait()
 
 
 def per_device(gradients, moduli, diag_terms, counts, targets, compliance, neighbours, rhs):
@@ -305,11 +332,11 @@
     lam, stiff = pl.pallas_call(
         kernel,
         out_shape=(
-            jax.ShapeDtypeStruct((N, COLS), F32),
-            jax.ShapeDtypeStruct((N * N, COLS), F32),
+            pltpu.VMEM((N, 1, COLS), F32),
+            pltpu.VMEM((N * N, 1, COLS), F32),
         ),
-        in_specs=[pl.BlockSpec(memory_space=pl.ANY)] * 8,
-        out_specs=[pl.BlockSpec(memory_space=pl.ANY)] * 2,
+        in_specs=[pl.BlockSpec(memory_space=pltpu.HBM)] * 8,
+        out_specs=[pl.BlockSpec(memory_space=pltpu.VMEM)] * 2,
         scratch_shapes=[
             vmem((9, N, ELEMS), BF16),
             vmem((9, ELEMS), BF16),
@@ -317,7 +344,7 @@
             vmem((1, SUB), I32),
             vmem((1, ELEMS), I32),
             vmem((1, COLS), I32),
-            vmem((N, COLS)),
+            vmem((N, 1, COLS)),
             vmem((N * N, COLS)),
             vmem((N * N, COLS)),
             vmem((SLOT_ROWS, LANES_OF * ELEMS), BF16),
@@ -327,37 +354,38 @@
             vmem((SUB, ROWS_OF, COLS), I32),
             vmem((96, COLS)),
             vmem((96, COLS)),
-            vmem((N * N, COLS)),
-            vmem((N, COLS)),
+            vmem((8, COLS)),
             vmem((8, COLS)),
             vmem((ROW, 8, COLS)),
-            vmem((COL, 8, COLS)),
-            vmem((GRP, 8, COLS)),
+            vmem((COL * GRP, 8, COLS)),
             dma((8,)),
-            pltpu.SemaphoreType.REGULAR,
-            dma((2,)),
+            pltpu.SemaphoreType.REGULAR((COL,)),
             dma((2,)),
             dma,
             dma((2,)),
             dma((2,)),
             dma((2,)),
             dma((2,)),
-            dma((2,)),
         ],
         compiler_params=pltpu.CompilerParams(
-            collective_id=0, has_side_effects=True, vmem_limit_bytes=32 * 1024 * 1024
+            collective_id=0, has_side_effects=True, vmem_limit_bytes=20 * 1024 * 1024
         ),
     )(
-        gradients[:, :, 0, :],
-        moduli[:, 0, :],
-        diag_terms[:, 0, :],
-        counts[0],
-        targets,
-        compliance[:, 0, :],
-        neighbours[0],
-        rhs[:, 0, :],
-    )
-    return lam[:, None, :], stiff[:, None, :]
+        *(
+            pltpu.with_memory_space_constraint(operand, pltpu.HBM)
+            for operand in (
+                gradients[:, :, 0, :],
+                moduli[:, 0, :],
+                diag_terms[:, 0, :],
+                counts[0],
+                targets,
+                compliance[:, 0, :],
+                neighbours[0],
+                rhs,
+            )
+        )
+    )
+    return lam, stiff
 
 
 def solution(mesh):

time: 52 us -> 44.3 us (0.85)
  local copies, waits for them, and re-layouts: 5.1 us -> 1.23 us
  Pallas kernels: 46 us -> 42.2 us
    unnamed x19 -> x2, local copies, waits for them, and re-layouts: 5.1 us -> 1.23 us
    pallas_call x1, Pallas kernels: 46 us -> 42.2 us  [per_device(): pl.pallas_call(kernel, out_shape=(pltpu.VMEM((N, 1, COLS), F32), pltpu.VM...]
where the time goes in v2:
time: 44.3 us; the launch traced here: 44.1 us
  Pallas kernels  42.2 us (95%)
  local copies, waits for them, and re-layouts  1.23 us (3%)
  between operations  0.64 us (1%)
    pallas_call x1, Pallas kernels, per_device(): pl.pallas_call(kernel, out_shape=(pltpu.VMEM((N, 1, COLS), F32), pltpu.VM...  42.2 us
    unnamed x2, local copies, waits for them, and re-layouts  1.23 us

profile of v2, /device:TPU:1, one launch (start us, length us, event | category | flops | bytes accessed | tf_op | source)
XLA Modules:
  0.0 44.1 jit_solution(3176760652470883618)
XLA Ops:
  0.6 42.2 %shard_map.95 = (f32[12,1,128]{2,1,0:T(1,128)S(1)}, f32[144,1,128]{2,1,0:T(1,128)S(1)}) custom-call(bf16[9,12,512]{2,1,0:T(8,128)(2,1)} %bitcast.6, bf16[9,512]{1,0:T(8,128)(2,1)} %bitcast.8, bf16[12,512]{1,0:T(8,128)(2,1)} %bitcast.9, s32[1,128]{1,0:T(1,128)} %bitcast.10, s32[1,512]{1,0:T(1,128)} %targets.1, f32[144,128]{1,0:T(8,128)} %bitcast.7, ...), custom_call_target="tpu_custom_call" | custom-call | tf_op jit(solution)/shard_map/pallas_call | solution.py:332
  42.9 0.6 %copy.12 = f32[12,1,128]{2,1,0:T(1,128)} copy(f32[12,1,128]{2,1,0:T(1,128)S(1)} %get-tuple-element.2) | data formatting | bytes 12288
  43.5 0.6 %copy.13 = f32[144,1,128]{2,1,0:T(1,128)} copy(f32[144,1,128]{2,1,0:T(1,128)S(1)} %get-tuple-element.3) | data formatting | bytes 147456

commit v3 on v2

--- a/solution.py
+++ b/solution.py
@@ -29,7 +29,8 @@
     ((y, x) for y in range(COL) for x in range(GRP) if y or x),
     key=lambda s: -hops(s[0], COL) - hops(s[1], GRP),
 )
-ROWS_ORDER = list(range(1, COL))
+FIRST_ROW = 5
+ROW_ORDER = sorted(range(COL), key=lambda r: hops(r, COL))
 COL_STEPS = sorted(range(1, COL), key=lambda s: -hops(s, COL))
 
 
@@ -71,32 +72,25 @@
     return out
 
 
-def combine(slots, count):
-    row = lax.broadcasted_iota(I32, (8, COLS), 0)
-    top = slots[0, 4:5]
-    for i in range(1, count):
-        top = jnp.maximum(top, slots[i, 4:5])
-    total = None
-    for i in range(count):
-        term = weigh(slots[i], slots[i, 4:5] / top, row)
-        total = term if total is None else total + term
-    return jnp.where(row == 4, jnp.broadcast_to(top, (8, COLS)), total)
-
-
-def weigh(block, ratio, row):
-    ratio = jnp.broadcast_to(ratio, (8, COLS))
+def combine(rows):
+    lane = lax.broadcasted_iota(I32, rows.shape, 1)
+    units = jnp.sum(jnp.where(lane == 4, rows, 0.0), axis=1, keepdims=True)
+    units = jnp.broadcast_to(units, rows.shape)
+    top = jnp.max(units, axis=0, keepdims=True)
+    ratio = units / top
     square = ratio * ratio
-    factor = jnp.where(row == 1, ratio, jnp.where(row == 2, square, square * ratio))
-    return block * jnp.where(row == 0, 1.0, factor)
+    power = jnp.where(lane == 1, ratio, jnp.where(lane == 2, square, square * ratio))
+    total = jnp.sum(rows * jnp.where(lane == 0, 1.0, power), axis=0, keepdims=True)
+    return jnp.where(lane[:1] < 4, total, top)
 
 
 def kernel(
     grads, mods, diag, counts, targets, comp, neigh, rhs,
     lam_out, stiff_out,
     g_v, m_v, d_v, c_v, t_v, n_v, r_v, own_c, near_c,
-    sel, rhs_h, rhs_l, send, recv, half_own, half_near,
+    sel, bytes_of, send, recv, half_own, half_near,
     mine, row_sum, slots_a, slots_b,
-    in_sem, row_sems, comp_sems, local_sem, move_sems, half_sems, sem_a, sem_b,
+    in_sem, row_sems, comp_sems, sent_sem, arrived, half_sems, sem_a, sem_b,
 ):
     me, grp = lax.axis_index("sub"), lax.axis_index("grp")
     y, zc = me // ROW, me % ROW
@@ -115,21 +109,38 @@
     def greet(device):
         pl.semaphore_signal(barrier, inc=1, device_id=device, device_id_type=MESH)
 
-    for dz, dc in ROW_STEPS:
-        greet(at(dz=dz, dc=dc))
-    for dy in COL_STEPS:
-        greet(at(dy=dy))
-    for dx in range(1, GRP):
-        greet(at(dx=dx))
-
-    loads = [(grads, g_v), (mods, m_v), (diag, d_v), (counts, c_v), (targets, t_v),
-             (neigh, n_v), (rhs, r_v), (comp, own_c)]
+    steps = [(hops(dz, 8), dict(dz=dz, dc=dc)) for dz, dc in ROW_STEPS]
+    steps += [(hops(dy, COL), dict(dy=dy)) for dy in COL_STEPS]
+    steps = [step for _, step in sorted(steps, key=lambda s: -s[0])]
+    for step in steps[:9]:
+        greet(at(**step))
+    loads = [(counts, c_v), (grads, g_v), (mods, m_v), (diag, d_v), (targets, t_v),
+             (comp, own_c), (neigh, n_v), (rhs, r_v)]
     loads = [pltpu.make_async_copy(a, b, in_sem.at[i]) for i, (a, b) in enumerate(loads)]
     for copy in loads:
         copy.start()
-    for copy in loads[:5]:
+    for step in steps[9:]:
+        greet(at(**step))
+    for dx in (2, 1, 3):
+        greet(at(dx=dx))
+
+    loads[0].wait()
+    line = lax.broadcasted_iota(I32, (SLOT_ROWS, COLS), 0)
+    lane = lax.broadcasted_iota(I32, (SLOT_ROWS, COLS), 1)
+    per_peer = jnp.broadcast_to(c_v[...].astype(F32), (COLS, SUB)).astype(BF16)
+    first = dot_nt((lane < line // ROWS_OF).astype(F32).astype(BF16), per_peer)
+    listed = dot_nt((lane == line // ROWS_OF).astype(F32).astype(BF16), per_peer)
+    place = ((line % ROWS_OF) * LANES_OF).astype(F32)
+    lane_f = lane.astype(F32)
+    for j in range(LANES_OF):
+        wanted = jnp.where(place + j < listed, first + place + j, -1.0)
+        for t in range(ELEMS // COLS):
+            hit = jnp.where(wanted == lane_f + t * COLS, 1.0, 0.0)
+            sel[j, :, t * COLS : (t + 1) * COLS] = hit.astype(BF16)
+
+    for copy in loads[1:5]:
         copy.wait()
-
+    bytes_of[...] = jnp.zeros_like(bytes_of)
     mods_f = m_v[...].astype(F32)
     for t in range(ELEMS // COLS):
         here = pl.ds(t * COLS, COLS)
@@ -149,33 +160,27 @@
         for half, values in enumerate((high, low)):
             values = jnp.concatenate(values, axis=0)
             upper = jnp.floor(values * (1.0 / 256.0)) * 256.0
-            for piece, ref in ((upper, rhs_h), (values - upper, rhs_l)):
-                for j in range(LANES_OF):
-                    parts = [piece]
-                    if j:
-                        parts = [jnp.zeros((j * WORDS, COLS), F32)] + parts
-                    parts = parts + [jnp.zeros((COLS - (j + 1) * WORDS, COLS), F32)]
-                    ref[half * COLS : (half + 1) * COLS, pl.ds(j * ELEMS + t * COLS, COLS)] = (
-                        jnp.concatenate(parts, axis=0).astype(BF16)
-                    )
-
-    line = lax.broadcasted_iota(I32, (SLOT_ROWS, COLS), 0)
-    lane = lax.broadcasted_iota(I32, (SLOT_ROWS, COLS), 1)
-    per_peer = jnp.broadcast_to(c_v[...].astype(F32), (COLS, SUB)).astype(BF16)
-    first = dot_nt((lane < line // ROWS_OF).astype(F32).astype(BF16), per_peer)
-    listed = dot_nt((lane == line // ROWS_OF).astype(F32).astype(BF16), per_peer)
-    place = ((line % ROWS_OF) * LANES_OF).astype(F32)
-    lane_f = lane.astype(F32)
-    for j in range(LANES_OF):
-        wanted = jnp.where(place + j < listed, first + place + j, -1.0)
-        for t in range(ELEMS // COLS):
-            hit = jnp.where(wanted == lane_f + t * COLS, 1.0, 0.0)
-            sel[:, pl.ds(j * ELEMS + t * COLS, COLS)] = hit.astype(BF16)
+            both = jnp.concatenate([upper, values - upper], axis=0)
+            bytes_of[half * COLS : half * COLS + 2 * WORDS, here] = both.astype(BF16)
+
+    lane = lax.broadcasted_iota(I32, (COLS, COLS), 1)
+    for c in range(4):
+        rows = pl.ds(c * COLS, COLS)
+        words = None
+        for j in range(LANES_OF):
+            found = dot_nt(sel[j, rows, :], bytes_of[...])
+            high, low = (
+                (half + pltpu.roll(half, COLS - WORDS, 1)).astype(I32)
+                for half in (found[:, :COLS], found[:, COLS:])
+            )
+            word = jnp.where(lane < WORDS, (high << 16) | (low & 0xFFFF), 0)
+            words = word if j == 0 else words | pltpu.roll(word, j * WORDS, 1)
+        send[pl.ds(c * 32, 32)] = words.reshape(32, ROWS_OF, COLS)
 
     pl.semaphore_wait(barrier, ROW + COL + GRP - 3)
     for dy in COL_STEPS:
         pl.semaphore_signal(
-            row_sems.at[COL - dy], inc=1, device_id=at(dy=dy), device_id_type=MESH
+            row_sems.at[y], inc=1, device_id=at(dy=dy), device_id_type=MESH
         )
     for copy in loads[5:]:
         copy.wait()
@@ -184,31 +189,24 @@
     )
     comp_copy.start()
 
-    for c in range(4):
-        rows = pl.ds(c * 128, 128)
-        packed = dot_nt(sel[rows, :], rhs_h[...]) + dot_nt(sel[rows, :], rhs_l[...])
-        packed = packed.astype(I32)
-        words = (packed[:, :COLS] << 16) | (packed[:, COLS:] & 0xFFFF)
-        send[pl.ds(c * 32, 32)] = words.reshape(32, ROWS_OF, COLS)
-
-    local = pltpu.make_async_copy(send.at[me], recv.at[me], local_sem)
-    local.start()
-
-    def post(dy, dz, dc):
-        device = at(dy, dz, dc)
+    shifted = (y + FIRST_ROW) % COL
+    slot, group = shifted * ROW + zc, shifted // (COL // 2)
+    pltpu.make_async_copy(send.at[me], recv.at[slot], arrived.at[group]).start()
+
+    def post(device):
         pltpu.make_async_remote_copy(
-            send.at[device[0]], recv.at[me], move_sems.at[0], move_sems.at[1],
+            send.at[device[0]], recv.at[slot], sent_sem, arrived.at[group],
             device_id=device, device_id_type=MESH,
         ).start()
 
     for dy in COL_STEPS:
-        post(dy, 0, 0)
+        post(at(dy=dy))
     for dz, dc in ROW_STEPS:
-        post(0, dz, dc)
-    for dy in ROWS_ORDER:
-        pl.semaphore_wait(row_sems.at[dy], 1)
+        post(at(dz=dz, dc=dc))
+    for dy in reversed(COL_STEPS):
+        pl.semaphore_wait(row_sems.at[(y + dy) % COL], 1)
         for dz, dc in ROW_STEPS:
-            post(dy, dz, dc)
+            post(at(dy, dz, dc))
 
     comp_copy.wait()
     facing = jnp.broadcast_to(n_v[...], (8, COLS))
@@ -227,32 +225,32 @@
     unit = both_c[0:1]
     for a in range(1, N):
         unit = jnp.maximum(unit, both_c[a * (N + 1) : a * (N + 1) + 1])
+    unit = jnp.max(unit, axis=1, keepdims=True)
     own_c[...] = both_c / unit
 
-    local.wait()
-    others = recv.at[pl.ds(0, SUB - 1)]
-    pltpu.make_async_copy(others, others, move_sems.at[1]).wait()
-
-    words = recv[...].reshape(SLOT_ROWS, COLS)
-    high = words >> 16
-    low = (words << 16) >> 16
-    pieces = [high >> 8, high & 255, low >> 8, low & 255]
-    pieces = jnp.concatenate([p.astype(F32).astype(BF16) for p in pieces], axis=1)
-    meta = low.astype(F32).T
-    patch = lax.broadcasted_iota(I32, (COLS, SLOT_ROWS), 0).astype(F32)
     lane = lax.broadcasted_iota(I32, (COLS, COLS), 1)
+    patch = lax.broadcasted_iota(I32, (COLS, SLOT_ROWS // 2), 0).astype(F32)
     sums = [jnp.zeros((COLS, COLS), F32)] * 2
-    for j in range(LANES_OF):
-        target = meta[j * WORDS + 36 : j * WORDS + 37]
-        code = meta[j * WORDS + 37 : j * WORDS + 38]
-        step = jnp.where(code < 0.0, code + 65536.0, code) * (1.0 / 512.0)
-        hit = jnp.where(patch == target, step, 0.0).astype(BF16)
-        part = jnp.dot(hit, pieces, preferred_element_type=F32)
-        here = (lane >= j * WORDS) & (lane < (j + 1) * WORDS)
-        for half in range(2):
-            upper = part[:, half * 256 : half * 256 + 128]
-            lower = part[:, half * 256 + 128 : half * 256 + 256]
-            sums[half] = sums[half] + jnp.where(here, upper * 256.0 + lower, 0.0)
+    for group in (1, 0):
+        block = recv.at[pl.ds(group * (SUB // 2), SUB // 2)]
+        pltpu.make_async_copy(block, block, arrived.at[group]).wait()
+        words = block[...].reshape(SLOT_ROWS // 2, COLS)
+        high = words >> 16
+        low = (words << 16) >> 16
+        pieces = [high >> 8, high & 255, low >> 8, low & 255]
+        pieces = jnp.concatenate([p.astype(F32).astype(BF16) for p in pieces], axis=1)
+        meta = low.astype(F32).T
+        for j in range(LANES_OF):
+            target = meta[j * WORDS + 36 : j * WORDS + 37]
+            code = meta[j * WORDS + 37 : j * WORDS + 38]
+            step = jnp.where(code < 0.0, code + 65536.0, code) * (1.0 / 512.0)
+            hit = jnp.where(patch == target, step, 0.0).astype(BF16)
+            part = jnp.dot(hit, pieces, preferred_element_type=F32)
+            here = (lane >= j * WORDS) & (lane < (j + 1) * WORDS)
+            for half in range(2):
+                upper = part[:, half * 256 : half * 256 + 128]
+                lower = part[:, half * 256 + 128 : half * 256 + 256]
+                sums[half] = sums[half] + jnp.where(here, upper * 256.0 + lower, 0.0)
     for half in range(2):
         turned = sums[half].T * (1.0 / 32768.0)
         folded = turned[:WORDS] + turned[WORDS : 2 * WORDS] + turned[2 * WORDS : 3 * WORDS]
@@ -284,10 +282,16 @@
     def inner(a, b):
         return jnp.sum(a * b, axis=0, keepdims=True)
 
-    mine[...] = jnp.concatenate(
+    totals = jnp.concatenate(
         [inner(resid, precond), inner(precond, image), inner(image, again),
-         inner(again, image_again), unit, jnp.zeros((3, COLS), F32)], axis=0,
-    )
+         inner(again, image_again)], axis=0,
+    )
+    totals = jnp.sum(totals, axis=1, keepdims=True)
+    lane = lax.broadcasted_iota(I32, (1, COLS), 1)
+    line = jnp.broadcast_to(unit, (1, COLS))
+    for i in range(4):
+        line = jnp.where(lane == i, totals[i : i + 1], line)
+    mine[...] = line
 
     def spread(source, slots, here, steps, sems):
         count = len(steps) + 1
@@ -299,7 +303,7 @@
             ).start()
         rest = slots.at[pl.ds(0, count - 1)]
         pltpu.make_async_copy(rest, rest, sems.at[1]).wait()
-        return combine(slots, count)
+        return combine(slots[:, 0, :])
 
     def sent(slots, steps, sems):
         rest = slots.at[pl.ds(0, len(steps))]
@@ -309,10 +313,9 @@
     fan_steps = [dict(dy=dy, dx=dx) for dy, dx in FAN_STEPS]
     row_sum[...] = spread(mine, slots_a, zc, row_steps, sem_a)
     total = spread(row_sum, slots_b, y * GRP + grp, fan_steps, sem_b)
-    row = lax.broadcasted_iota(I32, (8, COLS), 0)
-    top = jnp.max(total[4:5], axis=1, keepdims=True)
-    total = jnp.sum(weigh(total, total[4:5] / top, row), axis=1, keepdims=True)
-    rz, pq, quq, uw = (total[i : i + 1] for i in range(4))
+    rz, pq, quq, uw, top = (
+        jnp.sum(jnp.where(lane == i, total, 0.0), axis=1, keepdims=True) for i in range(5)
+    )
     alpha = rz / pq
     rz_next = alpha * alpha * quq - rz
     grown = 1.0 + rz_next / rz
@@ -323,7 +326,8 @@
     )
     sent(slots_a, row_steps, sem_a)
     sent(slots_b, fan_steps, sem_b)
-    pltpu.make_async_copy(others, others, move_sems.at[0]).wait()
+    others = recv.at[pl.ds(0, SUB - 1)]
+    pltpu.make_async_copy(others, others, sent_sem).wait()
 
 
 def per_device(gradients, moduli, diag_terms, counts, targets, compliance, neighbours, rhs):
@@ -347,17 +351,16 @@
             vmem((N, 1, COLS)),
             vmem((N * N, COLS)),
             vmem((N * N, COLS)),
-            vmem((SLOT_ROWS, LANES_OF * ELEMS), BF16),
-            vmem((2 * COLS, LANES_OF * ELEMS), BF16),
-            vmem((2 * COLS, LANES_OF * ELEMS), BF16),
+            vmem((LANES_OF, SLOT_ROWS, ELEMS), BF16),
+            vmem((2 * COLS, ELEMS), BF16),
             vmem((SUB, ROWS_OF, COLS), I32),
             vmem((SUB, ROWS_OF, COLS), I32),
             vmem((96, COLS)),
             vmem((96, COLS)),
-            vmem((8, COLS)),
-            vmem((8, COLS)),
-            vmem((ROW, 8, COLS)),
-            vmem((COL * GRP, 8, COLS)),
+            vmem((1, COLS)),
+            vmem((1, COLS)),
+            vmem((ROW, 1, COLS)),
+            vmem((COL * GRP, 1, COLS)),
             dma((8,)),
             pltpu.SemaphoreType.REGULAR((COL,)),
             dma((2,)),
@@ -385,7 +388,31 @@
             )
         )
     )
-    return lam, stiff
+    return pl.pallas_call(
+        place,
+        out_shape=(
+            jax.ShapeDtypeStruct((N, 1, COLS), F32),
+            jax.ShapeDtypeStruct((N * N, 1, COLS), F32),
+        ),
+        in_specs=[pl.BlockSpec(memory_space=pltpu.VMEM)] * 2,
+        out_specs=[pl.BlockSpec(memory_space=pl.ANY)] * 2,
+        scratch_shapes=[dma((2,))],
+        compiler_params=pltpu.CompilerParams(vmem_limit_bytes=20 * 1024 * 1024),
+    )(
+        pltpu.with_memory_space_constraint(lam, pltpu.VMEM),
+        pltpu.with_memory_space_constraint(stiff, pltpu.VMEM),
+    )
+
+
+def place(lam, stiff, lam_out, stiff_out, sems):
+    copies = [
+        pltpu.make_async_copy(stiff, stiff_out, sems.at[0]),
+        pltpu.make_async_copy(lam, lam_out, sems.at[1]),
+    ]
+    for copy in copies:
+        copy.start()
+    for copy in copies:
+        copy.wait()
 
 
 def solution(mesh):

time: 44.3 us -> 41.9 us (0.946)
  local copies, waits for them, and re-layouts: 1.23 us -> 0 us
  Pallas kernels: 42.2 us -> 41.1 us
    pallas_call x1, Pallas kernels: 42.2 us -> 40.5 us  [per_device(): pl.pallas_call(kernel, out_shape=(pltpu.VMEM((N, 1, COLS), F32), pltpu.VM...]
    unnamed x2 -> x0, local copies, waits for them, and re-layouts: 1.23 us -> none
    pallas_call x0 -> x1, Pallas kernels: none -> 0.65 us  [per_device(): pl.pallas_call(place, out_shape=(jax.ShapeDtypeStruct((N, 1, COLS), F32),...]
where the time goes in v3:
time: 41.9 us; the launch traced here: 41.8 us
  Pallas kernels  41.1 us (98%)
  between operations  0.64 us (2%)
    pallas_call x1, Pallas kernels, per_device(): pl.pallas_call(kernel, out_shape=(pltpu.VMEM((N, 1, COLS), F32), pltpu.VM...  40.5 us

profile of v3, /device:TPU:1, one launch (start us, length us, event | category | flops | bytes accessed | tf_op | source)
XLA Modules:
  0.0 41.8 jit_solution(18065060355846365865)
XLA Ops:
  0.6 40.5 %shard_map.95 = (f32[12,1,128]{2,1,0:T(1,128)S(1)}, f32[144,1,128]{2,1,0:T(1,128)S(1)}) custom-call(bf16[9,12,512]{2,1,0:T(8,128)(2,1)} %bitcast.6, bf16[9,512]{1,0:T(8,128)(2,1)} %bitcast.8, bf16[12,512]{1,0:T(8,128)(2,1)} %bitcast.9, s32[1,128]{1,0:T(1,128)} %bitcast.10, s32[1,512]{1,0:T(1,128)} %targets.1, f32[144,128]{1,0:T(8,128)} %bitcast.7, ...), custom_call_target="tpu_custom_call" | custom-call | tf_op jit(solution)/shard_map/pallas_call | solution.py:336
  41.1 0.7 %shard_map.96 = (f32[12,1,128]{2,1,0:T(1,128)}, f32[144,1,128]{2,1,0:T(1,128)}) custom-call(f32[12,1,128]{2,1,0:T(1,128)S(1)} %get-tuple-element.4.lam, f32[144,1,128]{2,1,0:T(1,128)S(1)} %get-tuple-element.5.stiff), custom_call_target="tpu_custom_call" | custom-call | tf_op jit(solution)/shard_map/pallas_call | solution.py:391

commit v4 on v3

--- a/solution.py
+++ b/solution.py
@@ -29,9 +29,9 @@
     ((y, x) for y in range(COL) for x in range(GRP) if y or x),
     key=lambda s: -hops(s[0], COL) - hops(s[1], GRP),
 )
-FIRST_ROW = 5
-ROW_ORDER = sorted(range(COL), key=lambda r: hops(r, COL))
 COL_STEPS = sorted(range(1, COL), key=lambda s: -hops(s, COL))
+SERVED = [0] + COL_STEPS[::-1]
+EARLY = 6
 
 
 def dot_nt(a, b):
@@ -189,24 +189,23 @@
     )
     comp_copy.start()
 
-    shifted = (y + FIRST_ROW) % COL
-    slot, group = shifted * ROW + zc, shifted // (COL // 2)
-    pltpu.make_async_copy(send.at[me], recv.at[slot], arrived.at[group]).start()
-
-    def post(device):
+    pltpu.make_async_copy(send.at[me], recv.at[zc], arrived.at[0]).start()
+
+    def post(dy, dz, dc):
+        device, place = at(dy, dz, dc), SERVED.index(dy)
         pltpu.make_async_remote_copy(
-            send.at[device[0]], recv.at[slot], sent_sem, arrived.at[group],
-            device_id=device, device_id_type=MESH,
+            send.at[device[0]], recv.at[place * ROW + zc], sent_sem,
+            arrived.at[0 if place < EARLY else 1], device_id=device, device_id_type=MESH,
         ).start()
 
     for dy in COL_STEPS:
-        post(at(dy=dy))
+        post(dy, 0, 0)
     for dz, dc in ROW_STEPS:
-        post(at(dz=dz, dc=dc))
-    for dy in reversed(COL_STEPS):
+        post(0, dz, dc)
+    for dy in SERVED[1:]:
         pl.semaphore_wait(row_sems.at[(y + dy) % COL], 1)
         for dz, dc in ROW_STEPS:
-            post(at(dy, dz, dc))
+            post(dy, dz, dc)
 
     comp_copy.wait()
     facing = jnp.broadcast_to(n_v[...], (8, COLS))
@@ -229,12 +228,13 @@
     own_c[...] = both_c / unit
 
     lane = lax.broadcasted_iota(I32, (COLS, COLS), 1)
-    patch = lax.broadcasted_iota(I32, (COLS, SLOT_ROWS // 2), 0).astype(F32)
     sums = [jnp.zeros((COLS, COLS), F32)] * 2
-    for group in (1, 0):
-        block = recv.at[pl.ds(group * (SUB // 2), SUB // 2)]
+    for group, rows in enumerate((EARLY, COL - EARLY)):
+        lines = rows * ROW * ROWS_OF
+        block = recv.at[pl.ds(group * EARLY * ROW, rows * ROW)]
         pltpu.make_async_copy(block, block, arrived.at[group]).wait()
-        words = block[...].reshape(SLOT_ROWS // 2, COLS)
+        words = block[...].reshape(lines, COLS)
+        patch = lax.broadcasted_iota(I32, (COLS, lines), 0).astype(F32)
         high = words >> 16
         low = (words << 16) >> 16
         pieces = [high >> 8, high & 255, low >> 8, low & 255]

time: 41.9 us -> 41.5 us (level)
  no operation moved by 1% of the time
where the time goes in v4:
time: 41.5 us; the launch traced here: 41.4 us
  Pallas kernels  40.7 us (98%)
  between operations  0.64 us (2%)
    pallas_call x1, Pallas kernels, per_device(): pl.pallas_call(kernel, out_shape=(pltpu.VMEM((N, 1, COLS), F32), pltpu.VM...  40.1 us

profile of v4, /device:TPU:1, one launch (start us, length us, event | category | flops | bytes accessed | tf_op | source)
XLA Modules:
  0.0 41.4 jit_solution(18068023359451042838)
XLA Ops:
  0.6 40.1 %shard_map.95 = (f32[12,1,128]{2,1,0:T(1,128)S(1)}, f32[144,1,128]{2,1,0:T(1,128)S(1)}) custom-call(bf16[9,12,512]{2,1,0:T(8,128)(2,1)} %bitcast.6, bf16[9,512]{1,0:T(8,128)(2,1)} %bitcast.8, bf16[12,512]{1,0:T(8,128)(2,1)} %bitcast.9, s32[1,128]{1,0:T(1,128)} %bitcast.10, s32[1,512]{1,0:T(1,128)} %targets.1, f32[144,128]{1,0:T(8,128)} %bitcast.7, ...), custom_call_target="tpu_custom_call" | custom-call | tf_op jit(solution)/shard_map/pallas_call | solution.py:336
  40.7 0.7 %shard_map.96 = (f32[12,1,128]{2,1,0:T(1,128)}, f32[144,1,128]{2,1,0:T(1,128)}) custom-call(f32[12,1,128]{2,1,0:T(1,128)S(1)} %get-tuple-element.4.lam, f32[144,1,128]{2,1,0:T(1,128)S(1)} %get-tuple-element.5.stiff), custom_call_target="tpu_custom_call" | custom-call | tf_op jit(solution)/shard_map/pallas_call | solution.py:391

commit v5 on v4

--- a/solution.py
+++ b/solution.py
@@ -202,9 +202,14 @@
         post(dy, 0, 0)
     for dz, dc in ROW_STEPS:
         post(0, dz, dc)
-    for dy in SERVED[1:]:
+    for dy in SERVED[1:EARLY]:
         pl.semaphore_wait(row_sems.at[(y + dy) % COL], 1)
         for dz, dc in ROW_STEPS:
+            post(dy, dz, dc)
+    for dy in SERVED[EARLY:]:
+        pl.semaphore_wait(row_sems.at[(y + dy) % COL], 1)
+    for dz, dc in ROW_STEPS:
+        for dy in SERVED[:EARLY - 1:-1]:
             post(dy, dz, dc)
 
     comp_copy.wait()

time: 41.5 us -> 41.4 us (level)
  no operation moved by 1% of the time
where the time goes in v5:
time: 41.4 us; the launch traced here: 41.3 us
  Pallas kernels  40.7 us (98%)
  between operations  0.64 us (2%)
    pallas_call x1, Pallas kernels, per_device(): pl.pallas_call(kernel, out_shape=(pltpu.VMEM((N, 1, COLS), F32), pltpu.VM...  40 us

profile of v5, /device:TPU:1, one launch (start us, length us, event | category | flops | bytes accessed | tf_op | source)
XLA Modules:
  0.0 41.3 jit_solution(18048811535807347977)
XLA Ops:
  0.6 40.0 %shard_map.95 = (f32[12,1,128]{2,1,0:T(1,128)S(1)}, f32[144,1,128]{2,1,0:T(1,128)S(1)}) custom-call(bf16[9,12,512]{2,1,0:T(8,128)(2,1)} %bitcast.6, bf16[9,512]{1,0:T(8,128)(2,1)} %bitcast.8, bf16[12,512]{1,0:T(8,128)(2,1)} %bitcast.9, s32[1,128]{1,0:T(1,128)} %bitcast.10, s32[1,512]{1,0:T(1,128)} %targets.1, f32[144,128]{1,0:T(8,128)} %bitcast.7, ...), custom_call_target="tpu_custom_call" | custom-call | tf_op jit(solution)/shard_map/pallas_call | solution.py:341
  40.7 0.7 %shard_map.96 = (f32[12,1,128]{2,1,0:T(1,128)}, f32[144,1,128]{2,1,0:T(1,128)}) custom-call(f32[12,1,128]{2,1,0:T(1,128)S(1)} %get-tuple-element.4.lam, f32[144,1,128]{2,1,0:T(1,128)S(1)} %get-tuple-element.5.stiff), custom_call_target="tpu_custom_call" | custom-call | tf_op jit(solution)/shard_map/pallas_call | solution.py:396
